TPU v7x, 32 devices: a whole 2x2x4 slice. The times are simulated.
32 devices in a mesh: ctx: 16 (over z, y, x), head: 2 (over core).
Axes of the slice: x: 2, y: 2, z: 4, core: 2. Of those that a mesh axis runs over, the one named last changes fastest.
Arguments:
- queries: bfloat16 [1024, 16, 576], P('ctx', 'head'), may hold values from -48 to 48
- latent: bfloat16 [1024, 576], P('ctx'), may hold values from -9 to 9
- w_uv: bfloat16 [16, 512, 128], P('head'), may hold values from -0.25 to 0.25
- w_out: bfloat16 [2048, 3584], P('ctx', 'head'), may hold values from -0.125 to 0.125
- pair_perm: int32 [16], replicated, may hold values from 0 to 15, each once
Outputs:
- mixed: bfloat16 [1024, 3584], P('ctx', 'head')
Inputs may be any that keep to these rules, and one draw needn't show every extreme that they name: `pair_perm`: a permutation of the span pairs.
All inputs are finite; a program needn't handle non-finite values.
Results may differ from a plain program's by a relative error of at most 0.0075.
Values may be sent and summed in bfloat16 or wider, within the bound.
A program may use at most 64 MiB of HBM per device.

v0:
```python
import jax
import jax.numpy as jnp
from jax import lax
from jax.sharding import PartitionSpec as P

LAT = 512
VDIM = 128


score_scale = 192.0 ** (-0.5)
block_rows = 512


def span_positions(pair_perm, offset, length, tok_dev, ctx_size):
    row_ids = offset + jnp.arange(length, dtype=jnp.int32)
    holder = row_ids // tok_dev
    within = row_ids % tok_dev
    device_ids = jnp.arange(ctx_size, dtype=jnp.int32)
    pair_ids = jnp.sum(
        jnp.where(holder[:, None] == device_ids[None, :], pair_perm[None, :], 0), axis=1
    )
    span_len = tok_dev // 2
    span_ids = jnp.where(within >= span_len, 2 * ctx_size - 1 - pair_ids, pair_ids)
    return span_ids * span_len + within % span_len


def attend(carried, query_rows, query_pos, key_rows, key_pos):
    ceiling, mass_sum, numerator = carried
    scores = (
        jnp.einsum("thd,kd->htk", query_rows, key_rows, preferred_element_type=jnp.float32)
        * score_scale
    )
    visible = key_pos[None, None, :] <= query_pos[None, :, None]
    scores = jnp.where(visible, scores, -1e30)
    raised = jnp.maximum(ceiling, jnp.max(scores, axis=2))
    shrink = jnp.exp(ceiling - raised)
    weights = jnp.where(visible, jnp.exp(scores - raised[:, :, None]), 0.0)
    mass_sum = mass_sum * shrink + jnp.sum(weights, axis=2)
    numerator = numerator * shrink[:, :, None] + jnp.einsum(
        "htk,kl->htl",
        weights.astype(jnp.bfloat16),
        key_rows[:, :LAT],
        preferred_element_type=jnp.float32,
    )
    return (raised, mass_sum, numerator)


def over_blocks(carried, portion, key_pos, step):
    length = portion.shape[0]
    blocks = length // block_rows
    lead_keys = portion.reshape(blocks, block_rows, portion.shape[1])
    lead_pos = key_pos.reshape(blocks, block_rows)

    def advance(current, block_in):
        return (step(current, block_in[0], block_in[1]), None)

    carried, _ = lax.scan(advance, carried, (lead_keys, lead_pos))
    return carried


def body(queries, latent, w_uv, w_out, pair_perm):
    tok_dev = queries.shape[0]
    heads_here = queries.shape[1]
    ctx_size = lax.axis_size("ctx")
    ctx_rank = lax.axis_index("ctx")
    query_pos = span_positions(pair_perm, ctx_rank * tok_dev, tok_dev, tok_dev, ctx_size)

    def fold_keys(carried, portion, offset):
        key_pos = span_positions(pair_perm, offset, portion.shape[0], tok_dev, ctx_size)

        def step(current, key_rows, key_ids):
            return attend(current, queries, query_pos, key_rows, key_ids)

        return over_blocks(carried, portion, key_pos, step)

    initial = (
        jnp.full((heads_here, tok_dev), -1e30, jnp.float32),
        jnp.zeros((heads_here, tok_dev), jnp.float32),
        jnp.zeros((heads_here, tok_dev, LAT), jnp.float32),
    )
    folded = fold_keys(initial, lax.all_gather(latent, "ctx", axis=0, tiled=True), jnp.int32(0))
    mass_sum = folded[1]
    numerator = folded[2]
    context = (numerator / mass_sum[:, :, None]).astype(jnp.bfloat16)
    values = jnp.einsum("htl,hlv->thv", context, w_uv, preferred_element_type=jnp.float32).astype(
        jnp.bfloat16
    )
    values = values.reshape(tok_dev, heads_here * VDIM)
    all_values = lax.all_gather(values, "head", axis=1, tiled=True)
    mixed = jnp.dot(
        all_values,
        lax.all_gather(w_out, "ctx", axis=0, tiled=True),
        preferred_element_type=jnp.float32,
    )
    return mixed.astype(jnp.bfloat16)


def solution(mesh):
    placed = (P("ctx", "head", None), P("ctx", None), P("head", None, None), P("ctx", "head"), P())
    return jax.shard_map(
        body, mesh=mesh, in_specs=placed, out_specs=P("ctx", "head"), check_vma=False
    )
```

profile of v0, /device:TPU:0, one launch (start us, length us, event | category | flops | bytes accessed | tf_op | source)
XLA Modules:
  0.0 186.7 jit_solution(9708230320540268902)
XLA Ops:
  6.5 0.7 all-gather.3.cloned.1.call-update
  7.3 0.0 all-gather.5.cloned.1.call-start
  7.3 0.7 all-gather.5.cloned.1.call-update
  8.0 2.0 %copy.16 = bf16[64,8,576]{2,0,1:T(8,128)(2,1)} copy(bf16[64,8,576]{2,1,0:T(8,128)(2,1)} %param.7) | data formatting | bytes 1179648
  10.1 0.0 copy-done.1
  10.1 0.1 select_reduce_fusion
  10.2 0.1 select_reduce_fusion.1
  10.3 59.4 %all-gather.3.cloned.1.call-done = bf16[1024,576]{1,0:T(8,128)(2,1)} async-done(((bf16[64,576]{1,0:T(8,128)(2,1)}), bf16[1024,576]{1,0:T(8,128)(2,1)}) %all-gather.3.cloned.1.call-update) | async-done | bytes 1179664 | tf_op jit(solution)/shard_map/all_gather | solution.py:81
  69.7 2.4 %copy.15 = bf16[2,512,576]{1,2,0:T(8,128)(2,1)} copy(bf16[2,512,576]{2,1,0:T(8,128)(2,1)} %bitcast.36) | data formatting | bytes 2359296
  72.1 8.2 %while.15 = (s32[]{:T(128)}, f32[8,64]{1,0:T(8,128)S(1)}, f32[8,64]{1,0:T(8,128)S(1)}, f32[8,64,512]{2,1,0:T(8,128)S(1)}, s32[2,512]{1,0:T(2,128)S(1)}, /*index=...) while((s32[]{:T(128)}, f32[8,64]{1,0:T(8,128)S(1)}, ...), condition=%wide.region_5.6_spmd.clone, body=%wide.region_2.5_spmd.clone.sunk | while | flops 573606400 | bytes 8366969 | solution.py:57
  72.1 0.1 broadcast_compare_fusion.2
  72.2 1.9 %fusion.36 = (f32[8,64]{1,0:T(8,128)S(1)}, f32[8,64,512]{2,1,0:T(8,128)S(1)}) fusion(bf16[64,8,576]{2,0,1:T(8,128)(2,1)} %get-tuple-element.205, bf16[2,512,576]{1,2,0:T(8,128)(2,1)} %get-tuple-element.204, s32[]{:T(128)} %get-tuple-element.188, pred[64,512]{1,0:T(8,128)(4,1)S(1)} %broadcast_compare_fusion.2), kind=kOutput, calls=%fused_computation.63.clone.1 | convolution fusion | flops 302775808 | bytes 2329088 | tf_op jit(solution)/shard_map/while/body/eval_jaxpr/thd,kd->htk/dot_general | solution.py:30
  74.2 0.4 fusion.37
  74.5 1.1 dynamic-slice_bitcast_fusion.2
  75.6 0.5 convolution_add_fusion.2
  76.2 0.1 broadcast_compare_fusion.2
  76.3 1.9 %fusion.36 = (f32[8,64]{1,0:T(8,128)S(1)}, f32[8,64,512]{2,1,0:T(8,128)S(1)}) fusion(bf16[64,8,576]{2,0,1:T(8,128)(2,1)} %get-tuple-element.205, bf16[2,512,576]{1,2,0:T(8,128)(2,1)} %get-tuple-element.204, s32[]{:T(128)} %get-tuple-element.188, pred[64,512]{1,0:T(8,128)(4,1)S(1)} %broadcast_compare_fusion.2), kind=kOutput, calls=%fused_computation.63.clone.1 | convolution fusion | flops 302775808 | bytes 2329088 | tf_op jit(solution)/shard_map/while/body/eval_jaxpr/thd,kd->htk/dot_general | solution.py:30
  78.2 0.4 fusion.37
  78.6 1.1 dynamic-slice_bitcast_fusion.2
  79.8 0.5 convolution_add_fusion.2
  80.3 0.4 fusion.13
  80.7 2.0 %all_gather.10 = bf16[64,2048]{1,0:T(8,128)(2,1)S(1)} all-gather(bf16[64,1024]{1,0:T(8,128)(2,1)S(1)} %bitcast.37), channel_id=1, replica_groups=mesh['ctx'=16,'head'=2] {'head'}, dimensions={1}, use_global_device_ids=true | all-gather | bytes 393216 | tf_op jit(solution)/shard_map/all_gather | solution.py:89
  82.7 92.0 %all-gather.5.cloned.1.call-done = bf16[2048,1792]{1,0:T(8,128)(2,1)} async-done(((bf16[128,1792]{1,0:T(8,128)(2,1)}), bf16[2048,1792]{1,0:T(8,128)(2,1)}) %all-gather.5.cloned.1.call-update) | async-done | bytes 7340048 | tf_op jit(solution)/shard_map/all_gather | solution.py:92
  174.8 5.1 %convolution_convert_fusion = bf16[64,1792]{1,0:T(8,128)(2,1)} fusion(bf16[64,2048]{1,0:T(8,128)(2,1)S(1)} %all_gather.10, bf16[2048,1792]{1,0:T(8,128)(2,1)} %all-gather.5.cloned.1.call-done), kind=kOutput, calls=%fused_computation.23 | convolution fusion | flops 469876736 | bytes 7831552 | tf_op jit(solution)/shard_map/dot_general | solution.py:90
  (21 shorter events, 0.2 us)
Async XLA Ops:
  6.5 73.8 %copy-start = (bf16[8,512,128]{2,1,0:T(8,128)(2,1)S(1)}, bf16[8,512,128]{2,1,0:T(8,128)(2,1)}, u32[]{:S(2)}) copy-start(bf16[8,512,128]{2,1,0:T(8,128)(2,1)} %param.9) | copy-start | bytes 3145732
  6.5 3.5 %copy-start.1 = (s32[16]{0:T(128)S(1)}, s32[16]{0:T(128)}, u32[]{:S(2)}) copy-start(s32[16]{0:T(128)} %param.11) | copy-start | bytes 196
  6.5 63.1 %all-gather.3.cloned.1.call-start = ((), (), s32[]{:S(2)}) async-start(), calls=%async_computation | async-start | bytes 1392640 | tf_op jit(solution)/shard_map/all_gather | solution.py:81
  7.3 167.5 %all-gather.5.cloned.1.call-start = ((), (), s32[]{:S(2)}) async-start(), calls=%async_computation.1 | async-start | bytes 7798784 | tf_op jit(solution)/shard_map/all_gather | solution.py:92
Sparse Core Ops, SparseCore 0:
  10.1 59.5 all-gather.2
  72.4 102.3 all-gather.4
where the time goes:
time: 187 us
  waiting for transfers between devices  153 us (82%)
  between operations  13.5 us (7%)
  matrix products  10.4 us (6%)
  local copies, waits for them, and re-layouts  6.73 us (4%)
  blocking collectives  1.99 us (1%)
    all_gather x1, waiting for transfers between devices, body(): lax.all_gather(w_out, 'ctx', axis=0, tiled=True)  92 us
    all_gather x1, waiting for transfers between devices, body(): lax.all_gather(latent, 'ctx', axis=0, tiled=True)  59.4 us
    dot_general x1, matrix products, body(): jnp.dot(all_values, lax.all_gather(w_out, 'ctx', axis=0, tiled=True), pre...  5.13 us
    unnamed x6, local copies, waits for them, and re-layouts  4.42 us
    dot_general x2, matrix products, attend(): jnp.einsum('thd,kd->htk', query_rows, key_rows, preferred_element_type=jn...  3.86 us
  transfers between devices with their start and end apart: 2, of which 2 were waited for; matrix products, arithmetic and copies ran while one was open for 7% of the time, Pallas kernels for 0%

commit v1 on v0

v1 whole, which is shorter than its diff:
```python
import functools

import jax
import jax.numpy as jnp
from jax import lax
from jax.experimental import pallas as pl
from jax.experimental.pallas import tpu as pltpu
from jax.sharding import PartitionSpec as P

LAT = 512
VDIM = 128
MESH = pl.DeviceIdType.MESH

score_scale = 192.0 ** (-0.5)


def split_ctx(n_ctx):
    low = 1
    while low * low < n_ctx:
        low *= 2
    return n_ctx // low, low


def kernel(
    dims,
    perm_ref,
    lat_ref,
    q_hbm,
    uv_hbm,
    w_hbm,
    out_ref,
    q_ref,
    uv_ref,
    lat,
    ctx_f32,
    w1,
    w2,
    vals1,
    vals2,
    x1,
    x2,
    part1,
    part2,
    send1,
    send2,
    got1,
    got2,
    local_sems,
    hi_send,
    hi_recv,
    lo_send,
    lo_recv,
    core_send,
    core_recv,
    w1_send,
    w1_recv,
    w2_send,
    w2_recv,
    v1_send,
    v1_recv,
    v2_send,
    v2_recv,
    r1_send,
    r1_recv,
    r2_send,
    r2_recv,
):
    n_hi, n_lo, n_head, tok, heads, cols1 = dims
    n_ctx = n_hi * n_lo
    ratio = heads // n_lo
    pieces = 2 if n_head == 2 else 1
    rows_piece = tok // pieces
    me = lax.axis_index("ctx")
    k = lax.axis_index("head")
    hi = me // n_lo
    lo = lax.rem(me, n_lo)

    def hi_at(d):
        return lax.rem(hi + (d + n_hi) % n_hi, n_hi)

    def lo_at(d):
        return lax.rem(lo + (d + n_lo) % n_lo, n_lo)

    def k_at(d):
        return lax.rem(k + (d + n_head) % n_head, n_head)

    def device(h, l, kk):
        return (h * n_lo + l, kk)

    def remote(src, dst, send, recv, target):
        return pltpu.make_async_remote_copy(
            src_ref=src,
            dst_ref=dst,
            send_sem=send,
            recv_sem=recv,
            device_id=target,
            device_id_type=MESH,
        )

    q_copy = pltpu.make_async_copy(q_hbm, q_ref, local_sems.at[0])
    uv_copy = pltpu.make_async_copy(uv_hbm, uv_ref, local_sems.at[1])
    w1_copy = pltpu.make_async_copy(
        w_hbm.at[:, pl.ds(0, cols1)],
        w1.at[pl.ds(pl.multiple_of(hi * VDIM, VDIM), VDIM), :],
        local_sems.at[2],
    )
    w2_copy = pltpu.make_async_copy(
        w_hbm.at[:, pl.ds(cols1, w_hbm.shape[1] - cols1)],
        w2.at[pl.ds(pl.multiple_of(lo * VDIM, VDIM), VDIM), :],
        local_sems.at[3],
    )

    partners = [(0, dl, dk) for dl in range(n_lo) for dk in range(n_head) if dl or dk]
    partners += [(dh, 0, dk) for dh in range(1, n_hi) for dk in range(n_head)]
    barrier = pltpu.get_barrier_semaphore()
    for dh, dl, dk in partners:
        pl.semaphore_signal(
            barrier,
            inc=1,
            device_id=device(hi_at(dh), lo_at(dl), k_at(dk)),
            device_id_type=MESH,
        )
    lat[pl.ds(pl.multiple_of(me * tok, tok), tok), :] = lat_ref[...]
    pl.semaphore_wait(barrier, len(partners))

    def piece(dh, dl, kk):
        owner = hi_at(-dh) * n_lo + lo_at(-dl)
        start = owner * tok
        if pieces > 1:
            start = start + kk * rows_piece
        return lat.at[pl.ds(pl.multiple_of(start, rows_piece), rows_piece), :]

    own = piece(0, 0, k)
    sent = []

    def start(copy):
        copy.start()
        sent.append(copy)

    def to_hi(d):
        return remote(own, own, hi_send.at[d], hi_recv.at[d], device(hi_at(d), lo, k))

    def to_lo(dh, d):
        block = piece(dh, 0, k)
        return remote(
            block, block, lo_send.at[dh, d], lo_recv.at[dh, d], device(hi, lo_at(d), k)
        )

    def to_core(dh, dl):
        block = piece(dh, dl, k)
        return remote(
            block, block, core_send.at[dh, dl], core_recv.at[dh, dl], device(hi, lo, k_at(1))
        )

    def arrived(block, recv):
        remote(block, block, recv, recv, device(hi, lo, k_at(1))).wait_recv()

    for d in range(1, n_hi):
        start(to_hi(d))
    for d in range(1, n_lo):
        start(to_lo(0, d))
    for d in range(1, n_lo):
        start(
            remote(
                w_hbm.at[:, pl.ds(cols1, w_hbm.shape[1] - cols1)],
                w2.at[pl.ds(pl.multiple_of(lo * VDIM, VDIM), VDIM), :],
                w2_send.at[d],
                w2_recv.at[d],
                device(hi, lo_at(d), k),
            )
        )
    for d in range(1, n_hi):
        start(
            remote(
                w_hbm.at[:, pl.ds(0, cols1)],
                w1.at[pl.ds(pl.multiple_of(hi * VDIM, VDIM), VDIM), :],
                w1_send.at[d],
                w1_recv.at[d],
                device(hi_at(d), lo, k),
            )
        )
    for copy in (q_copy, uv_copy, w1_copy, w2_copy):
        copy.start()
    for d in range(1, n_hi):
        arrived(piece(d, 0, k), hi_recv.at[d])
        for e in range(1, n_lo):
            start(to_lo(d, e))
        if pieces > 1:
            start(to_core(d, 0))
    for dh in range(n_hi):
        for dl in range(1, n_lo):
            arrived(piece(dh, dl, k), lo_recv.at[dh, dl])
            if pieces > 1:
                start(to_core(dh, dl))

    total = n_ctx * tok
    half = tok // 2
    key_ids = lax.broadcasted_iota(jnp.int32, (1, total), 1)
    holder = key_ids // tok
    pair = jnp.zeros((1, total), jnp.int32)
    for c in range(n_ctx):
        pair = jnp.where(holder == c, perm_ref[c], pair)
    within = lax.rem(key_ids, tok)
    key_pos = jnp.where(within >= half, 2 * n_ctx - 1 - pair, pair) * half + lax.rem(within, half)
    my_pair = perm_ref[me]

    q_copy.wait()
    uv_copy.wait()
    if pieces > 1:
        for dh in range(n_hi):
            for dl in range(n_lo):
                if dh or dl:
                    arrived(piece(dh, dl, k_at(1)), core_recv.at[dh, dl])

    all_rows = tok * heads
    rows = 256 if total <= 1024 else 64
    for first in range(0, all_rows, rows):
        row_tok = (first + lax.broadcasted_iota(jnp.int32, (rows, 1), 0)) // heads
        query_pos = jnp.where(
            row_tok >= half, 2 * n_ctx - 1 - my_pair, my_pair
        ) * half + lax.rem(row_tok, half)
        scores = (
            lax.dot_general(
                q_ref[pl.ds(first, rows), :],
                lat[...],
                (((1,), (1,)), ((), ())),
                preferred_element_type=jnp.float32,
            )
            * score_scale
        )
        scores = jnp.where(key_pos <= query_pos, scores, -1e30)
        weights = jnp.exp(scores - jnp.max(scores, axis=1, keepdims=True))
        mass = jnp.sum(weights, axis=1, keepdims=True)
        numerator = jnp.dot(
            weights.astype(jnp.bfloat16), lat[:, pl.ds(0, LAT)], preferred_element_type=jnp.float32
        )
        context = numerator / mass
        for j in range(LAT // 128):
            ctx_f32[j, pl.ds(first, rows), :] = context[:, j * 128 : (j + 1) * 128]

    for h in range(heads):
        context = jnp.concatenate(
            [ctx_f32[j, pl.ds(h, tok, stride=heads), :] for j in range(LAT // 128)], axis=1
        ).astype(jnp.bfloat16)
        value = jnp.dot(context, uv_ref[h], preferred_element_type=jnp.float32).astype(jnp.bfloat16)
        r, l = h // n_lo, h % n_lo
        vals1[l, :, pl.ds(r * VDIM, VDIM)] = value
        vals2[r, :, pl.ds(l * VDIM, VDIM)] = value

    owner_k = hi // ratio
    mine = k == owner_k

    @pl.when(mine)
    def _():
        x2[hi] = vals2[lax.rem(hi, ratio)]

    def x2_copy(r, dk):
        return remote(
            vals2.at[r],
            x2.at[hi],
            v2_send.at[r, dk],
            v2_recv.at[hi],
            device(k * ratio + r, lo, k_at(dk)),
        )

    for r in range(ratio):
        for dk in range(n_head):
            if dk:
                x2_copy(r, dk).start()
            else:

                @pl.when(k * ratio + r != hi)
                def _():
                    x2_copy(r, 0).start()

    x1[lo, k] = vals1[lo]
    for dl in range(n_lo):
        for dk in range(n_head):
            if dl or dk:
                start(
                    remote(
                        vals1.at[lo_at(dl)],
                        x1.at[lo, k],
                        v1_send.at[dl, dk],
                        v1_recv.at[dl, dk],
                        device(hi, lo_at(dl), k_at(dk)),
                    )
                )

    w2_copy.wait()
    for d in range(1, n_lo):
        arrived(
            w2.at[pl.ds(pl.multiple_of(lo_at(-d) * VDIM, VDIM), VDIM), :], w2_recv.at[d]
        )
    for z in range(n_hi):

        @pl.when(jnp.logical_not(jnp.logical_and(mine, hi == z)))
        def _():
            arrived(x2.at[z], v2_recv.at[z])

    product = jnp.dot(
        x2[...].reshape(n_hi * tok, n_lo * VDIM), w2[...], preferred_element_type=jnp.float32
    )
    part2[...] = product.reshape(part2.shape)
    send2[...] = product.astype(jnp.bfloat16).reshape(send2.shape)
    for d in range(1, n_hi):
        start(
            remote(
                send2.at[hi_at(d)],
                got2.at[d],
                r2_send.at[d],
                r2_recv.at[d],
                device(hi_at(d), lo, k),
            )
        )

    w1_copy.wait()
    for d in range(1, n_hi):
        arrived(
            w1.at[pl.ds(pl.multiple_of(hi_at(-d) * VDIM, VDIM), VDIM), :], w1_recv.at[d]
        )
    for dl in range(n_lo):
        for dk in range(n_head):
            if dl or dk:
                arrived(x1.at[lo_at(-dl), k_at(-dk)], v1_recv.at[dl, dk])
    product = None
    depth = ratio * VDIM
    for kk in range(n_head):
        term = jnp.dot(
            x1[:, kk].reshape(n_lo * tok, depth),
            w1[pl.ds(kk * depth, depth), :],
            preferred_element_type=jnp.float32,
        )
        product = term if product is None else product + term
    part1[...] = product.reshape(part1.shape)
    send1[...] = product.astype(jnp.bfloat16).reshape(send1.shape)
    for d in range(1, n_lo):
        start(
            remote(
                send1.at[lo_at(d)],
                got1.at[d],
                r1_send.at[d],
                r1_recv.at[d],
                device(hi, lo_at(d), k),
            )
        )

    mixed = part1[lo]
    for d in range(1, n_lo):
        arrived(got1.at[d], r1_recv.at[d])
        mixed = mixed + got1[d].astype(jnp.float32)
    out_ref[:, pl.ds(0, cols1)] = mixed.astype(jnp.bfloat16)
    mixed = part2[hi]
    for d in range(1, n_hi):
        arrived(got2.at[d], r2_recv.at[d])
        mixed = mixed + got2[d].astype(jnp.float32)
    out_ref[:, pl.ds(cols1, out_ref.shape[1] - cols1)] = mixed.astype(jnp.bfloat16)

    for copy in sent:
        copy.wait_send()
    for r in range(ratio):
        for dk in range(n_head):
            if dk:
                x2_copy(r, dk).wait_send()
            else:

                @pl.when(k * ratio + r != hi)
                def _():
                    x2_copy(r, 0).wait_send()


def body(n_ctx, n_head, queries, latent, w_uv, w_out, pair_perm):
    n_hi, n_lo = split_ctx(n_ctx)
    tok, heads, width = queries.shape
    ratio = heads // n_lo
    columns = w_out.shape[1]
    cols1 = columns // 256 * 128
    cols2 = columns - cols1
    dims = (n_hi, n_lo, n_head, tok, heads, cols1)
    bf16, f32 = jnp.bfloat16, jnp.float32
    vmem, dma = pltpu.VMEM, pltpu.SemaphoreType.DMA
    anywhere = pl.BlockSpec(memory_space=pl.ANY)
    return pl.pallas_call(
        functools.partial(kernel, dims),
        out_shape=jax.ShapeDtypeStruct((tok, columns), bf16),
        in_specs=[
            pl.BlockSpec(memory_space=pltpu.SMEM),
            pl.BlockSpec(memory_space=vmem),
            anywhere,
            anywhere,
            anywhere,
        ],
        out_specs=pl.BlockSpec(memory_space=vmem),
        scratch_shapes=[
            vmem((tok * heads, width), bf16),
            vmem(w_uv.shape, bf16),
            vmem((n_ctx * tok, width), bf16),
            vmem((LAT // 128, tok * heads, 128), f32),
            vmem((n_hi * VDIM, cols1), bf16),
            vmem((n_lo * VDIM, cols2), bf16),
            vmem((n_lo, tok, ratio * VDIM), bf16),
            vmem((ratio, tok, n_lo * VDIM), bf16),
            vmem((n_lo, n_head, tok, ratio * VDIM), bf16),
            vmem((n_hi, tok, n_lo * VDIM), bf16),
            vmem((n_lo, tok, cols1), f32),
            vmem((n_hi, tok, cols2), f32),
            vmem((n_lo, tok, cols1), bf16),
            vmem((n_hi, tok, cols2), bf16),
            vmem((n_lo, tok, cols1), bf16),
            vmem((n_hi, tok, cols2), bf16),
            dma((4,)),
            dma((n_hi,)),
            dma((n_hi,)),
            dma((n_hi, n_lo)),
            dma((n_hi, n_lo)),
            dma((n_hi, n_lo)),
            dma((n_hi, n_lo)),
            dma((n_hi,)),
            dma((n_hi,)),
            dma((n_lo,)),
            dma((n_lo,)),
            dma((n_lo, n_head)),
            dma((n_lo, n_head)),
            dma((ratio, n_head)),
            dma((n_hi,)),
            dma((n_lo,)),
            dma((n_lo,)),
            dma((n_hi,)),
            dma((n_hi,)),
        ],
        compiler_params=pltpu.CompilerParams(
            collective_id=0, has_side_effects=True, vmem_limit_bytes=56 * 1024 * 1024
        ),
    )(pair_perm, latent, queries.reshape(tok * heads, width), w_uv, w_out)


def solution(mesh):
    placed = (P("ctx", "head", None), P("ctx", None), P("head", None, None), P("ctx", "head"), P())
    return jax.shard_map(
        functools.partial(body, mesh.shape["ctx"], mesh.shape["head"]),
        mesh=mesh,
        in_specs=placed,
        out_specs=P("ctx", "head"),
        check_vma=False,
    )
```

time: 187 us -> 49.7 us (0.27)
  waiting for transfers between devices: 153 us -> 0 us
  Pallas kernels: 0 us -> 47.8 us
  between operations: 13.5 us -> 0.01 us
  matrix products: 10.4 us -> 0 us
  local copies, waits for them, and re-layouts: 6.73 us -> 1.64 us
  blocking collectives: 1.99 us -> 0 us
    all_gather x2 -> x0, waiting for transfers between devices: 151 us -> none  [the longest x1 92 us: body(): lax.all_gather(w_out, 'ctx', axis=0, tiled=True)]
    pallas_call x0 -> x1, Pallas kernels: none -> 47.8 us  [body(): pl.pallas_call(functools.partial(kernel, dims), out_shape=jax.ShapeDtypeS...]
    dot_general x6 -> x0, matrix products: 10.4 us -> none  [the longest x1 5.13 us: body(): jnp.dot(all_values, lax.all_gather(w_out, 'ctx', axis=0, tiled=True), pre...]
    unnamed x6 -> x1, local copies, waits for them, and re-layouts: 4.42 us -> 1.64 us
    squeeze x2 -> x0, local copies, waits for them, and re-layouts: 2.26 us -> none  [over_blocks(): carried, _ = lax.scan(advance, carried, (lead_keys, lead_pos))]
    all_gather x1 -> x0, blocking collectives: 1.99 us -> none  [body(): all_values = lax.all_gather(values, 'head', axis=1, tiled=True)]
  transfers between devices with their start and end apart: 2 -> 0, of which waited for: 2 -> 0; matrix products, arithmetic and copies ran while one was open for 7% -> 0% of each run, Pallas kernels for 0% -> 0%
where the time goes in v1:
time: 49.7 us; the launch traced here: 49.5 us
  Pallas kernels  47.8 us (96%)
  local copies, waits for them, and re-layouts  1.64 us (3%)
    pallas_call x1, Pallas kernels, body(): pl.pallas_call(functools.partial(kernel, dims), out_shape=jax.ShapeDtypeS...  47.8 us
    unnamed x1, local copies, waits for them, and re-layouts  1.64 us

profile of v1, /device:TPU:0, one launch (start us, length us, event | category | flops | bytes accessed | tf_op | source)
XLA Modules:
  0.0 49.5 jit_solution(7039803689105083180)
XLA Ops:
  0.0 47.8 %shard_map.55 = bf16[64,1792]{1,0:T(8,128)(2,1)} custom-call(s32[16]{0:T(128)} %perm_ref.1, bf16[64,576]{1,0:T(8,128)(2,1)} %lat_ref.1, bf16[512,576]{1,0:T(8,128)(2,1)} %bitcast.1, bf16[8,512,128]{2,1,0:T(8,128)(2,1)} %uv_hbm.1, bf16[128,1792]{1,0:T(8,128)(2,1)} %w_hbm.1), custom_call_target="tpu_custom_call" | custom-call | tf_op jit(solution)/shard_map/pallas_call | solution.py:383
  47.8 1.6 %copy.7 = bf16[64,1792]{1,0:T(8,128)(2,1)} copy(bf16[64,1792]{1,0:T(8,128)(2,1)} %shard_map.55) | data formatting | bytes 458752

commit v2 on v1

--- a/solution.py
+++ b/solution.py
@@ -59,13 +59,14 @@
     v1_send,
     v1_recv,
     v2_send,
+    vf_send,
     v2_recv,
     r1_send,
     r1_recv,
     r2_send,
     r2_recv,
 ):
-    n_hi, n_lo, n_head, tok, heads, cols1 = dims
+    n_hi, n_lo, n_head, tok, heads, cols1, chunks1, chunks2 = dims
     n_ctx = n_hi * n_lo
     ratio = heads // n_lo
     pieces = 2 if n_head == 2 else 1
@@ -159,26 +160,12 @@
         start(to_hi(d))
     for d in range(1, n_lo):
         start(to_lo(0, d))
-    for d in range(1, n_lo):
-        start(
-            remote(
-                w_hbm.at[:, pl.ds(cols1, w_hbm.shape[1] - cols1)],
-                w2.at[pl.ds(pl.multiple_of(lo * VDIM, VDIM), VDIM), :],
-                w2_send.at[d],
-                w2_recv.at[d],
-                device(hi, lo_at(d), k),
-            )
-        )
-    for d in range(1, n_hi):
-        start(
-            remote(
-                w_hbm.at[:, pl.ds(0, cols1)],
-                w1.at[pl.ds(pl.multiple_of(hi * VDIM, VDIM), VDIM), :],
-                w1_send.at[d],
-                w1_recv.at[d],
-                device(hi_at(d), lo, k),
-            )
-        )
+    def w1_rows(source):
+        return w1.at[pl.ds(pl.multiple_of(source * VDIM, VDIM), VDIM), :]
+
+    def w2_rows(source):
+        return w2.at[pl.ds(pl.multiple_of(source * VDIM, VDIM), VDIM), :]
+
     for copy in (q_copy, uv_copy, w1_copy, w2_copy):
         copy.start()
     for d in range(1, n_hi):
@@ -187,6 +174,26 @@
             start(to_lo(d, e))
         if pieces > 1:
             start(to_core(d, 0))
+    for d in range(1, n_lo):
+        start(
+            remote(
+                w_hbm.at[:, pl.ds(cols1, w_hbm.shape[1] - cols1)],
+                w2_rows(lo),
+                w2_send.at[d],
+                w2_recv.at[d],
+                device(hi, lo_at(d), k),
+            )
+        )
+    for d in range(1, n_hi):
+        start(
+            remote(
+                w_hbm.at[:, pl.ds(0, cols1)],
+                w1_rows(hi),
+                w1_send.at[d],
+                w1_recv.at[d],
+                device(hi_at(d), lo, k),
+            )
+        )
     for dh in range(n_hi):
         for dl in range(1, n_lo):
             arrived(piece(dh, dl, k), lo_recv.at[dh, dl])
@@ -254,24 +261,26 @@
     def _():
         x2[hi] = vals2[lax.rem(hi, ratio)]
 
-    def x2_copy(r, dk):
+    def x2_copy(r):
         return remote(
-            vals2.at[r],
-            x2.at[hi],
-            v2_send.at[r, dk],
-            v2_recv.at[hi],
-            device(k * ratio + r, lo, k_at(dk)),
+            vals2.at[r], x2.at[hi], v2_send.at[r], v2_recv.at[hi], device(k * ratio + r, lo, k)
+        )
+
+    def x2_hand_on(z, dk):
+        return remote(
+            x2.at[z], x2.at[z], vf_send.at[z, dk], v2_recv.at[z], device(hi, lo, k_at(dk))
         )
 
     for r in range(ratio):
-        for dk in range(n_head):
-            if dk:
-                x2_copy(r, dk).start()
-            else:
-
-                @pl.when(k * ratio + r != hi)
-                def _():
-                    x2_copy(r, 0).start()
+
+        @pl.when(k * ratio + r != hi)
+        def _():
+            x2_copy(r).start()
+
+    @pl.when(mine)
+    def _():
+        for dk in range(1, n_head):
+            x2_hand_on(hi, dk).start()
 
     x1[lo, k] = vals1[lo]
     for dl in range(n_lo):
@@ -292,81 +301,93 @@
         arrived(
             w2.at[pl.ds(pl.multiple_of(lo_at(-d) * VDIM, VDIM), VDIM), :], w2_recv.at[d]
         )
-    for z in range(n_hi):
-
-        @pl.when(jnp.logical_not(jnp.logical_and(mine, hi == z)))
-        def _():
+    @pl.when(mine)
+    def _():
+        for d in range(1, n_hi):
+            z = hi_at(d)
             arrived(x2.at[z], v2_recv.at[z])
-
-    product = jnp.dot(
-        x2[...].reshape(n_hi * tok, n_lo * VDIM), w2[...], preferred_element_type=jnp.float32
-    )
-    part2[...] = product.reshape(part2.shape)
-    send2[...] = product.astype(jnp.bfloat16).reshape(send2.shape)
-    for d in range(1, n_hi):
-        start(
-            remote(
-                send2.at[hi_at(d)],
-                got2.at[d],
-                r2_send.at[d],
-                r2_recv.at[d],
-                device(hi_at(d), lo, k),
-            )
-        )
+            for dk in range(1, n_head):
+                x2_hand_on(z, dk).start()
+
+    @pl.when(jnp.logical_not(mine))
+    def _():
+        for z in range(n_hi):
+            arrived(x2.at[z], v2_recv.at[z])
+
+    rows2 = x2[...].reshape(n_hi * tok, n_lo * VDIM)
+    for c, (first, size) in enumerate(chunks2):
+        cols = pl.ds(first, size)
+        product = jnp.dot(rows2, w2[:, cols], preferred_element_type=jnp.float32)
+        product = product.reshape(n_hi, tok, size)
+        part2[:, :, cols] = product
+        send2[:, :, cols] = product.astype(jnp.bfloat16)
+        for d in range(1, n_hi):
+            start(
+                remote(
+                    send2.at[hi_at(d), :, cols],
+                    got2.at[d, :, cols],
+                    r2_send.at[c, d],
+                    r2_recv.at[c, d],
+                    device(hi_at(d), lo, k),
+                )
+            )
 
     w1_copy.wait()
     for d in range(1, n_hi):
-        arrived(
-            w1.at[pl.ds(pl.multiple_of(hi_at(-d) * VDIM, VDIM), VDIM), :], w1_recv.at[d]
-        )
+        arrived(w1_rows(hi_at(-d)), w1_recv.at[d])
     for dl in range(n_lo):
         for dk in range(n_head):
             if dl or dk:
                 arrived(x1.at[lo_at(-dl), k_at(-dk)], v1_recv.at[dl, dk])
-    product = None
     depth = ratio * VDIM
-    for kk in range(n_head):
-        term = jnp.dot(
-            x1[:, kk].reshape(n_lo * tok, depth),
-            w1[pl.ds(kk * depth, depth), :],
-            preferred_element_type=jnp.float32,
-        )
-        product = term if product is None else product + term
-    part1[...] = product.reshape(part1.shape)
-    send1[...] = product.astype(jnp.bfloat16).reshape(send1.shape)
-    for d in range(1, n_lo):
-        start(
-            remote(
-                send1.at[lo_at(d)],
-                got1.at[d],
-                r1_send.at[d],
-                r1_recv.at[d],
-                device(hi, lo_at(d), k),
-            )
-        )
-
-    mixed = part1[lo]
-    for d in range(1, n_lo):
-        arrived(got1.at[d], r1_recv.at[d])
-        mixed = mixed + got1[d].astype(jnp.float32)
-    out_ref[:, pl.ds(0, cols1)] = mixed.astype(jnp.bfloat16)
-    mixed = part2[hi]
-    for d in range(1, n_hi):
-        arrived(got2.at[d], r2_recv.at[d])
-        mixed = mixed + got2[d].astype(jnp.float32)
-    out_ref[:, pl.ds(cols1, out_ref.shape[1] - cols1)] = mixed.astype(jnp.bfloat16)
+    rows1 = [x1[:, kk].reshape(n_lo * tok, depth) for kk in range(n_head)]
+    for c, (first, size) in enumerate(chunks1):
+        cols = pl.ds(first, size)
+        product = None
+        for kk in range(n_head):
+            term = jnp.dot(
+                rows1[kk], w1[pl.ds(kk * depth, depth), cols], preferred_element_type=jnp.float32
+            )
+            product = term if product is None else product + term
+        product = product.reshape(n_lo, tok, size)
+        part1[:, :, cols] = product
+        send1[:, :, cols] = product.astype(jnp.bfloat16)
+        for d in range(1, n_lo):
+            start(
+                remote(
+                    send1.at[lo_at(d), :, cols],
+                    got1.at[d, :, cols],
+                    r1_send.at[c, d],
+                    r1_recv.at[c, d],
+                    device(hi, lo_at(d), k),
+                )
+            )
+
+    def add_up(part, mine_at, got, recv, chunks, n, base):
+        for c, (first, size) in enumerate(chunks):
+            cols = pl.ds(first, size)
+            mixed = part[mine_at, :, cols]
+            for d in range(1, n):
+                arrived(got.at[d, :, cols], recv.at[c, d])
+                mixed = mixed + got[d, :, cols].astype(jnp.float32)
+            out_ref[:, pl.ds(base + first, size)] = mixed.astype(jnp.bfloat16)
+
+    add_up(part1, lo, got1, r1_recv, chunks1, n_lo, 0)
+    add_up(part2, hi, got2, r2_recv, chunks2, n_hi, cols1)
 
     for copy in sent:
         copy.wait_send()
     for r in range(ratio):
-        for dk in range(n_head):
-            if dk:
-                x2_copy(r, dk).wait_send()
-            else:
-
-                @pl.when(k * ratio + r != hi)
-                def _():
-                    x2_copy(r, 0).wait_send()
+
+        @pl.when(k * ratio + r != hi)
+        def _():
+            x2_copy(r).wait_send()
+
+    @pl.when(mine)
+    def _():
+        for z in range(n_hi):
+            for dk in range(1, n_head):
+                x2_hand_on(z, dk).wait_send()
 
 
 def body(n_ctx, n_head, queries, latent, w_uv, w_out, pair_perm):
@@ -374,9 +395,10 @@
     tok, heads, width = queries.shape
     ratio = heads // n_lo
     columns = w_out.shape[1]
-    cols1 = columns // 256 * 128
+    cols1 = columns // 128 * 6 // 14 * 128
     cols2 = columns - cols1
-    dims = (n_hi, n_lo, n_head, tok, heads, cols1)
+    chunks1, chunks2 = [(0, cols1)], [(0, cols2)]
+    dims = (n_hi, n_lo, n_head, tok, heads, cols1, chunks1, chunks2)
     bf16, f32 = jnp.bfloat16, jnp.float32
     vmem, dma = pltpu.VMEM, pltpu.SemaphoreType.DMA
     anywhere = pl.BlockSpec(memory_space=pl.ANY)
@@ -421,12 +443,13 @@
             dma((n_lo,)),
             dma((n_lo, n_head)),
             dma((n_lo, n_head)),
-            dma((ratio, n_head)),
+            dma((ratio,)),
+            dma((n_hi, n_head)),
             dma((n_hi,)),
-            dma((n_lo,)),
-            dma((n_lo,)),
-            dma((n_hi,)),
-            dma((n_hi,)),
+            dma((len(chunks1), n_lo)),
+            dma((len(chunks1), n_lo)),
+            dma((len(chunks2), n_hi)),
+            dma((len(chunks2), n_hi)),
         ],
         compiler_params=pltpu.CompilerParams(
             collective_id=0, has_side_effects=True, vmem_limit_bytes=56 * 1024 * 1024

time: 49.7 us -> 48 us (0.966)
  Pallas kernels: 47.8 us -> 45.7 us
    pallas_call x1, Pallas kernels: 47.8 us -> 45.7 us  [body(): pl.pallas_call(functools.partial(kernel, dims), out_shape=jax.ShapeDtypeS...]
where the time goes in v2:
time: 48 us; the launch traced here: 47.4 us
  Pallas kernels  45.7 us (95%)
  local copies, waits for them, and re-layouts  1.64 us (3%)
    pallas_call x1, Pallas kernels, body(): pl.pallas_call(functools.partial(kernel, dims), out_shape=jax.ShapeDtypeS...  45.7 us
    unnamed x1, local copies, waits for them, and re-layouts  1.64 us

profile of v2, /device:TPU:0, one launch (start us, length us, event | category | flops | bytes accessed | tf_op | source)
XLA Modules:
  0.0 47.4 jit_solution(1996371427178576429)
XLA Ops:
  0.0 45.7 %shard_map.55 = bf16[64,1792]{1,0:T(8,128)(2,1)} custom-call(s32[16]{0:T(128)} %perm_ref.1, bf16[64,576]{1,0:T(8,128)(2,1)} %lat_ref.1, bf16[512,576]{1,0:T(8,128)(2,1)} %bitcast.1, bf16[8,512,128]{2,1,0:T(8,128)(2,1)} %uv_hbm.1, bf16[128,1792]{1,0:T(8,128)(2,1)} %w_hbm.1), custom_call_target="tpu_custom_call" | custom-call | tf_op jit(solution)/shard_map/pallas_call | solution.py:405
  45.7 1.6 %copy.7 = bf16[64,1792]{1,0:T(8,128)(2,1)} copy(bf16[64,1792]{1,0:T(8,128)(2,1)} %shard_map.55) | data formatting | bytes 458752

commit v3 on v2

--- a/solution.py
+++ b/solution.py
@@ -160,12 +160,44 @@
         start(to_hi(d))
     for d in range(1, n_lo):
         start(to_lo(0, d))
-    def w1_rows(source):
-        return w1.at[pl.ds(pl.multiple_of(source * VDIM, VDIM), VDIM), :]
-
-    def w2_rows(source):
-        return w2.at[pl.ds(pl.multiple_of(source * VDIM, VDIM), VDIM), :]
-
+    part_rows = VDIM // 2
+
+    def w1_rows(source, h):
+        start = source * VDIM + h * part_rows
+        return w1.at[pl.ds(pl.multiple_of(start, part_rows), part_rows), :]
+
+    def w2_rows(source, h):
+        start = source * VDIM + h * part_rows
+        return w2.at[pl.ds(pl.multiple_of(start, part_rows), part_rows), :]
+
+    def send_w1(h):
+        for d in range(1, n_hi):
+            start(
+                remote(
+                    w_hbm.at[pl.ds(h * part_rows, part_rows), pl.ds(0, cols1)],
+                    w1_rows(hi, h),
+                    w1_send.at[h, d],
+                    w1_recv.at[h, d],
+                    device(hi_at(d), lo, k),
+                )
+            )
+
+    def send_w2(h):
+        for d in range(1, n_lo):
+            start(
+                remote(
+                    w_hbm.at[
+                        pl.ds(h * part_rows, part_rows),
+                        pl.ds(cols1, w_hbm.shape[1] - cols1),
+                    ],
+                    w2_rows(lo, h),
+                    w2_send.at[h, d],
+                    w2_recv.at[h, d],
+                    device(hi, lo_at(d), k),
+                )
+            )
+
+    send_w1(0)
     for copy in (q_copy, uv_copy, w1_copy, w2_copy):
         copy.start()
     for d in range(1, n_hi):
@@ -174,26 +206,9 @@
             start(to_lo(d, e))
         if pieces > 1:
             start(to_core(d, 0))
-    for d in range(1, n_lo):
-        start(
-            remote(
-                w_hbm.at[:, pl.ds(cols1, w_hbm.shape[1] - cols1)],
-                w2_rows(lo),
-                w2_send.at[d],
-                w2_recv.at[d],
-                device(hi, lo_at(d), k),
-            )
-        )
-    for d in range(1, n_hi):
-        start(
-            remote(
-                w_hbm.at[:, pl.ds(0, cols1)],
-                w1_rows(hi),
-                w1_send.at[d],
-                w1_recv.at[d],
-                device(hi_at(d), lo, k),
-            )
-        )
+    send_w2(0)
+    send_w2(1)
+    send_w1(1)
     for dh in range(n_hi):
         for dl in range(1, n_lo):
             arrived(piece(dh, dl, k), lo_recv.at[dh, dl])
@@ -297,10 +312,9 @@
                 )
 
     w2_copy.wait()
-    for d in range(1, n_lo):
-        arrived(
-            w2.at[pl.ds(pl.multiple_of(lo_at(-d) * VDIM, VDIM), VDIM), :], w2_recv.at[d]
-        )
+    for h in range(2):
+        for d in range(1, n_lo):
+            arrived(w2_rows(lo_at(-d), h), w2_recv.at[h, d])
     @pl.when(mine)
     def _():
         for d in range(1, n_hi):
@@ -333,8 +347,9 @@
             )
 
     w1_copy.wait()
-    for d in range(1, n_hi):
-        arrived(w1_rows(hi_at(-d)), w1_recv.at[d])
+    for h in range(2):
+        for d in range(1, n_hi):
+            arrived(w1_rows(hi_at(-d), h), w1_recv.at[h, d])
     for dl in range(n_lo):
         for dk in range(n_head):
             if dl or dk:
@@ -437,10 +452,10 @@
             dma((n_hi, n_lo)),
             dma((n_hi, n_lo)),
             dma((n_hi, n_lo)),
-            dma((n_hi,)),
-            dma((n_hi,)),
-            dma((n_lo,)),
-            dma((n_lo,)),
+            dma((2, n_hi)),
+            dma((2, n_hi)),
+            dma((2, n_lo)),
+            dma((2, n_lo)),
             dma((n_lo, n_head)),
             dma((n_lo, n_head)),
             dma((ratio,)),

time: 48 us -> 46.8 us (0.975)
  Pallas kernels: 45.7 us -> 44.9 us
    pallas_call x1, Pallas kernels: 45.7 us -> 44.9 us  [body(): pl.pallas_call(functools.partial(kernel, dims), out_shape=jax.ShapeDtypeS...]
where the time goes in v3:
time: 46.8 us; the launch traced here: 46.6 us
  Pallas kernels  44.9 us (96%)
  local copies, waits for them, and re-layouts  1.64 us (4%)
    pallas_call x1, Pallas kernels, body(): pl.pallas_call(functools.partial(kernel, dims), out_shape=jax.ShapeDtypeS...  44.9 us
    unnamed x1, local copies, waits for them, and re-layouts  1.64 us

profile of v3, /device:TPU:0, one launch (start us, length us, event | category | flops | bytes accessed | tf_op | source)
XLA Modules:
  0.0 46.6 jit_solution(8742713608942375698)
XLA Ops:
  0.0 44.9 %shard_map.55 = bf16[64,1792]{1,0:T(8,128)(2,1)} custom-call(s32[16]{0:T(128)} %perm_ref.1, bf16[64,576]{1,0:T(8,128)(2,1)} %lat_ref.1, bf16[512,576]{1,0:T(8,128)(2,1)} %bitcast.1, bf16[8,512,128]{2,1,0:T(8,128)(2,1)} %uv_hbm.1, bf16[128,1792]{1,0:T(8,128)(2,1)} %w_hbm.1), custom_call_target="tpu_custom_call" | custom-call | tf_op jit(solution)/shard_map/pallas_call | solution.py:420
  45.0 1.6 %copy.7 = bf16[64,1792]{1,0:T(8,128)(2,1)} copy(bf16[64,1792]{1,0:T(8,128)(2,1)} %shard_map.55) | data formatting | bytes 458752

commit v4 on v3

--- a/solution.py
+++ b/solution.py
@@ -260,6 +260,11 @@
         for j in range(LAT // 128):
             ctx_f32[j, pl.ds(first, rows), :] = context[:, j * 128 : (j + 1) * 128]
 
+    def x2_copy(r):
+        return remote(
+            vals2.at[r], x2.at[hi], v2_send.at[r], v2_recv.at[hi], device(k * ratio + r, lo, k)
+        )
+
     for h in range(heads):
         context = jnp.concatenate(
             [ctx_f32[j, pl.ds(h, tok, stride=heads), :] for j in range(LAT // 128)], axis=1
@@ -268,6 +273,12 @@
         r, l = h // n_lo, h % n_lo
         vals1[l, :, pl.ds(r * VDIM, VDIM)] = value
         vals2[r, :, pl.ds(l * VDIM, VDIM)] = value
+        if l == n_lo - 1:
+
+            @pl.when(k * ratio + r != hi)
+            def _():
+                x2_copy(r).start()
+
 
     owner_k = hi // ratio
     mine = k == owner_k
@@ -276,21 +287,10 @@
     def _():
         x2[hi] = vals2[lax.rem(hi, ratio)]
 
-    def x2_copy(r):
-        return remote(
-            vals2.at[r], x2.at[hi], v2_send.at[r], v2_recv.at[hi], device(k * ratio + r, lo, k)
-        )
-
     def x2_hand_on(z, dk):
         return remote(
             x2.at[z], x2.at[z], vf_send.at[z, dk], v2_recv.at[z], device(hi, lo, k_at(dk))
         )
-
-    for r in range(ratio):
-
-        @pl.when(k * ratio + r != hi)
-        def _():
-            x2_copy(r).start()
 
     @pl.when(mine)
     def _():

time: 46.8 us -> 46.8 us (level)
  no operation moved by 1% of the time
where the time goes in v4:
time: 46.8 us; the launch traced here: 46.6 us
  Pallas kernels  44.9 us (96%)
  local copies, waits for them, and re-layouts  1.64 us (4%)
    pallas_call x1, Pallas kernels, body(): pl.pallas_call(functools.partial(kernel, dims), out_shape=jax.ShapeDtypeS...  44.9 us
    unnamed x1, local copies, waits for them, and re-layouts  1.64 us

profile of v4, /device:TPU:0, one launch (start us, length us, event | category | flops | bytes accessed | tf_op | source)
XLA Modules:
  0.0 46.6 jit_solution(4319601268121989250)
XLA Ops:
  0.0 44.9 %shard_map.55 = bf16[64,1792]{1,0:T(8,128)(2,1)} custom-call(s32[16]{0:T(128)} %perm_ref.1, bf16[64,576]{1,0:T(8,128)(2,1)} %lat_ref.1, bf16[512,576]{1,0:T(8,128)(2,1)} %bitcast.1, bf16[8,512,128]{2,1,0:T(8,128)(2,1)} %uv_hbm.1, bf16[128,1792]{1,0:T(8,128)(2,1)} %w_hbm.1), custom_call_target="tpu_custom_call" | custom-call | tf_op jit(solution)/shard_map/pallas_call | solution.py:420
  45.0 1.6 %copy.7 = bf16[64,1792]{1,0:T(8,128)(2,1)} copy(bf16[64,1792]{1,0:T(8,128)(2,1)} %shard_map.55) | data formatting | bytes 458752
